TPU v7x, 128 devices: a whole 4x4x4 slice. The times are simulated.
128 devices in a mesh: head: 4 (over z), doc: 32 (over y, x, core).
Axes of the slice: x: 4, y: 4, z: 4, core: 2. Of those that a mesh axis runs over, the one named last changes fastest.
Arguments:
- packed_query_rows: bfloat16 [16384, 4096], P(('doc', 'head')), may hold values from -160 to 160
- packed_key_rows: bfloat16 [16384, 1024], P(('doc', 'head')), may hold values from -6 to 6
- packed_value_rows: bfloat16 [16384, 1024], P(('doc', 'head')), may hold values from -6 to 6
- doc_lengths: int32 [64], replicated, may hold values from 1 to 2048, 16384 in all
Outputs:
- attended: bfloat16 [16384, 4096], P(('doc', 'head'))
Inputs may be any that keep to these rules, and one draw needn't show every extreme that they name: `doc_lengths`: the documents lie end to end in order and their lengths sum to 16384.
All inputs are finite; a program needn't handle non-finite values.
Results may differ from a plain program's by a relative error of at most 0.011.
Values may be sent and summed in bfloat16 or wider, within the bound.
A program may use at most 64 MiB of HBM per device.

v0:
```python
import functools
import math

import jax
import jax.numpy as jnp
from jax import lax
from jax.experimental import pallas as pl
from jax.experimental.pallas import tpu as pltpu
from jax.sharding import PartitionSpec as P

HEAD_SIZE = 128
GROUP = 4
TILE = 128
CHIP_TILES = 8
WINDOW_TILES = 24
REACH = 16
DOCS = 64
SCALE = math.log2(math.e) / math.sqrt(HEAD_SIZE)
HIDDEN = -1e30
MESH = pl.DeviceIdType.MESH
RELAY_FROM = 3
WIDE = 256


def kernel(
    lens_ref, q_ref, k_ref, v_ref, o_ref,
    qb, kvb, relay, feat_q, feat_k, s_scr, p_scr, ob,
    q_send, q_recv, k_send, k_recv, v_send, v_recv,
    x1_send, x1_recv, x2_send, x2_recv, relay_send, relay_recv, o_send, o_recv,
):
    z = lax.axis_index("head")
    d = lax.axis_index("doc")
    core = lax.rem(d, 2)
    c = lax.div(d, 2)
    x = lax.rem(c, 4)
    y = lax.div(c, 4)
    my_tile = core * 4 + z
    my_head = z * 2 + core

    def chip(yy, xx):
        return (lax.rem(yy + 4, 4) * 4 + lax.rem(xx + 4, 4)) * 2 + core

    ahead = lax.rem(d + 2, 32)
    behind = lax.rem(d + 30, 32)
    relay_to = chip(y, x - 1)
    relay_source = chip(y, x + 1)
    crossing = jnp.where((x == 1) | (x == 2), 1, 0)
    final_to = chip(y + crossing, x - 1)
    sender_crossing = jnp.where((x == 0) | (x == 1), 1, 0)
    final_from = chip(y - sender_crossing, x + 1)

    def column(g):
        return {"head": lax.div(g, 2), "doc": c * 2 + lax.rem(g, 2)}

    def along(dd):
        return {"head": z, "doc": dd}

    barrier = pltpu.get_barrier_semaphore()

    def greet(i, _):
        g = lax.rem(my_head + i, 8)
        pl.semaphore_signal(barrier, inc=1, device_id=column(g), device_id_type=MESH)
        return 0

    lax.fori_loop(1, 8, greet, 0)
    for other in (behind, relay_source, final_from):
        pl.semaphore_signal(barrier, inc=1, device_id=along(other), device_id_type=MESH)
    pl.semaphore_wait(barrier, 10)

    def rows(tile, count=1):
        return pl.ds(pl.multiple_of(tile * TILE, TILE), TILE * count)

    def cols(g, width):
        return pl.ds(pl.multiple_of(g * width, width), width)

    def k_copy(g, tile):
        return pltpu.make_async_remote_copy(
            src_ref=k_ref.at[:, cols(g, HEAD_SIZE)],
            dst_ref=kvb.at[0, rows(REACH + tile), :],
            send_sem=k_send.at[g], recv_sem=k_recv.at[tile],
            device_id=column(g), device_id_type=MESH)

    def v_copy(g, tile):
        return pltpu.make_async_remote_copy(
            src_ref=v_ref.at[:, cols(g, HEAD_SIZE)],
            dst_ref=kvb.at[1, rows(REACH + tile), :],
            send_sem=v_send.at[g], recv_sem=v_recv.at[tile],
            device_id=column(g), device_id_type=MESH)

    def q_copy(g, tile):
        return pltpu.make_async_remote_copy(
            src_ref=q_ref.at[:, cols(g, GROUP * HEAD_SIZE)],
            dst_ref=qb.at[tile],
            send_sem=q_send.at[g], recv_sem=q_recv.at[tile],
            device_id=column(g), device_id_type=MESH)

    def x1_copy(j):
        return pltpu.make_async_remote_copy(
            src_ref=kvb.at[:, rows(16 + j), :],
            dst_ref=kvb.at[:, rows(8 + j), :],
            send_sem=x1_send.at[j], recv_sem=x1_recv.at[j],
            device_id=along(ahead), device_id_type=MESH)

    def x2_copy(j):
        return pltpu.make_async_remote_copy(
            src_ref=kvb.at[:, rows(8 + j), :],
            dst_ref=kvb.at[:, rows(j), :],
            send_sem=x2_send.at[j], recv_sem=x2_recv.at[j],
            device_id=along(ahead), device_id_type=MESH)

    def relay_copy(j):
        return pltpu.make_async_remote_copy(
            src_ref=kvb.at[:, rows(16 + j), :],
            dst_ref=relay.at[j - RELAY_FROM],
            send_sem=relay_send.at[j], recv_sem=relay_recv.at[j],
            device_id=along(relay_to), device_id_type=MESH)

    def final_copy(j):
        return pltpu.make_async_remote_copy(
            src_ref=relay.at[j - RELAY_FROM],
            dst_ref=kvb.at[:, rows(j), :],
            send_sem=x2_send.at[j], recv_sem=x2_recv.at[j],
            device_id=along(final_to), device_id_type=MESH)

    def o_copy(g, tile):
        target = {"head": lax.rem(tile, 4), "doc": c * 2 + lax.div(tile, 4)}
        return pltpu.make_async_remote_copy(
            src_ref=ob.at[tile],
            dst_ref=o_ref.at[:, cols(g, GROUP * HEAD_SIZE)],
            send_sem=o_send.at[tile], recv_sem=o_recv.at[g],
            device_id=target, device_id_type=MESH)

    def send_kv(i, _):
        g = lax.rem(my_head + i, 8)
        k_copy(g, my_tile).start()
        v_copy(g, my_tile).start()
        return 0

    def send_q(i, _):
        g = lax.rem(my_head + i, 8)
        q_copy(g, my_tile).start()
        return 0

    lax.fori_loop(1, 8, send_kv, 0)
    pltpu.make_async_copy(
        k_ref.at[:, cols(my_head, HEAD_SIZE)], kvb.at[0, rows(REACH + my_tile), :], k_recv.at[my_tile]
    ).start()
    pltpu.make_async_copy(
        v_ref.at[:, cols(my_head, HEAD_SIZE)], kvb.at[1, rows(REACH + my_tile), :], v_recv.at[my_tile]
    ).start()
    lax.fori_loop(1, 8, send_q, 0)
    pltpu.make_async_copy(
        q_ref.at[:, cols(my_head, GROUP * HEAD_SIZE)], qb.at[my_tile], q_recv.at[my_tile]
    ).start()

    lane = lax.broadcasted_iota(jnp.int32, (1, 128), 1)

    def add_document(i, bounds):
        first, end = bounds
        length = lens_ref[i]
        return first + jnp.where(lane > i, length, 0), end + jnp.where(lane >= i, length, 0)

    zero = jnp.zeros((1, 128), jnp.int32)
    first, end = lax.fori_loop(0, DOCS, add_document, (zero, zero))
    first = jnp.where(lane == DOCS, -(1 << 30), first)
    end = jnp.where(lane == DOCS, 0, end)
    line = lax.broadcasted_iota(jnp.int32, (TILE, 128), 0)

    def member(tile):
        token = line + (c * CHIP_TILES - REACH + tile) * TILE
        return (token >= first) & (token < end)

    def key_features(tile, _):
        feat_k[rows(tile), :] = jnp.where(member(tile), 1.0, 0.0).astype(jnp.bfloat16)
        return 0

    def query_features(tile, _):
        feat_q[rows(tile), :] = jnp.where(member(tile + REACH), 0.0, HIDDEN).astype(jnp.bfloat16)
        return 0

    lax.fori_loop(0, WINDOW_TILES, key_features, 0)
    lax.fori_loop(0, CHIP_TILES, query_features, 0)

    def pass_own(t, _):
        j = CHIP_TILES - 1 - t
        k_copy(my_head, j).wait_recv()
        v_copy(my_head, j).wait_recv()
        x1_copy(j).start()

        @pl.when(j >= RELAY_FROM)
        def _():
            relay_copy(j).start()

        return 0

    lax.fori_loop(0, CHIP_TILES, pass_own, 0)

    def pass_on(t, _):
        j = CHIP_TILES - 1 - t
        x1_copy(j).wait_recv()

        @pl.when(j >= RELAY_FROM)
        def _():
            relay_copy(j).wait_recv()
            final_copy(j).start()

        @pl.when(j < RELAY_FROM)
        def _():
            x2_copy(j).start()

        return 0

    lax.fori_loop(0, CHIP_TILES, pass_on, 0)

    ones = jnp.ones(((REACH + 1) * TILE, 128), jnp.bfloat16)
    span = (REACH + 1) * TILE

    def attend(t, _):
        j = CHIP_TILES - 1 - t
        q_copy(my_head, j).wait_recv()
        x2_copy(j).wait_recv()
        queries = qb[j]
        features = feat_q[rows(j), :]
        left = jnp.concatenate(
            [queries[:, h * HEAD_SIZE:(h + 1) * HEAD_SIZE] for h in range(GROUP)], axis=0)
        left = jnp.concatenate([left, jnp.concatenate([features] * GROUP, axis=0)], axis=1)
        highest = None
        for at in range(0, span, WIDE):
            width = min(WIDE, span - at)
            part = pl.ds(pl.multiple_of(j * TILE + at, TILE), width)
            right = jnp.concatenate([kvb[0, part, :], feat_k[part, :]], axis=1)
            s = lax.dot_general(
                left, right, (((1,), (1,)), ((), ())), preferred_element_type=jnp.float32)
            if at + width == span:
                row = lax.rem(lax.broadcasted_iota(jnp.int32, s.shape, 0), TILE)
                col = lax.broadcasted_iota(jnp.int32, s.shape, 1) - (width - TILE)
                s = jnp.where(col <= row, s, HIDDEN)
            s_scr[:, at:at + width] = s
            for g in range(0, width, 128):
                piece = s[:, g:g + 128]
                highest = piece if highest is None else jnp.maximum(highest, piece)
        highest = jnp.max(highest, axis=1, keepdims=True)
        for at in range(0, span, WIDE):
            width = min(WIDE, span - at)
            p = jnp.exp2((s_scr[:, at:at + width] - highest) * SCALE)
            p_scr[:, at:at + width] = p.astype(jnp.bfloat16)
        values = jnp.concatenate([kvb[1, rows(j, REACH + 1), :], ones], axis=1)
        summed = jnp.dot(p_scr[...], values, preferred_element_type=jnp.float32)
        out = (summed[:, :HEAD_SIZE] / summed[:, HEAD_SIZE:]).astype(jnp.bfloat16)
        for h in range(GROUP):
            ob[j, :, h * HEAD_SIZE:(h + 1) * HEAD_SIZE] = out[h * TILE:(h + 1) * TILE]

        @pl.when(j != my_tile)
        def _():
            o_copy(my_head, j).start()

        @pl.when(j == my_tile)
        def _():
            pltpu.make_async_copy(
                ob.at[j], o_ref.at[:, cols(my_head, GROUP * HEAD_SIZE)], o_recv.at[my_head]
            ).start()

        return 0

    lax.fori_loop(0, CHIP_TILES, attend, 0)

    def finish(i, _):
        g = lax.rem(my_head + i, 8)
        o_copy(g, my_tile).wait_recv()
        x1_copy(i).wait_send()

        @pl.when(i >= RELAY_FROM)
        def _():
            relay_copy(i).wait_send()
            final_copy(i).wait_send()

        @pl.when(i < RELAY_FROM)
        def _():
            x2_copy(i).wait_send()

        @pl.when(i > 0)
        def _():
            k_copy(g, my_tile).wait_send()
            v_copy(g, my_tile).wait_send()
            q_copy(g, my_tile).wait_send()
            tile = lax.rem(my_tile + i, 8)
            o_copy(my_head, tile).wait_send()

        return 0

    lax.fori_loop(0, 8, finish, 0)


def on_device(packed_query_rows, packed_key_rows, packed_value_rows, doc_lengths):
    anywhere = pl.BlockSpec(memory_space=pl.ANY)
    bf16, f32 = jnp.bfloat16, jnp.float32
    dma = pltpu.SemaphoreType.DMA((8,))
    window = WINDOW_TILES * TILE
    span = (REACH + 1) * TILE
    return pl.pallas_call(
        kernel,
        out_shape=jax.ShapeDtypeStruct(packed_query_rows.shape, bf16),
        in_specs=[pl.BlockSpec(memory_space=pltpu.SMEM), anywhere, anywhere, anywhere],
        out_specs=anywhere,
        scratch_shapes=[
            pltpu.VMEM((CHIP_TILES, TILE, GROUP * HEAD_SIZE), bf16),
            pltpu.VMEM((2, window, HEAD_SIZE), bf16),
            pltpu.VMEM((CHIP_TILES - RELAY_FROM, 2, TILE, HEAD_SIZE), bf16),
            pltpu.VMEM((CHIP_TILES * TILE, 128), bf16),
            pltpu.VMEM((window, 128), bf16),
            pltpu.VMEM((GROUP * TILE, span), f32),
            pltpu.VMEM((GROUP * TILE, span), bf16),
            pltpu.VMEM((CHIP_TILES, TILE, GROUP * HEAD_SIZE), bf16),
        ] + [dma] * 14,
        compiler_params=pltpu.CompilerParams(
            collective_id=0, has_side_effects=True, vmem_limit_bytes=40 * 1024 * 1024),
        name="attention",
    )(doc_lengths, packed_query_rows, packed_key_rows, packed_value_rows)


def solution(mesh):
    token = P(("doc", "head"), None)
    return jax.shard_map(
        on_device, mesh=mesh, in_specs=(token, token, token, P()), out_specs=token, check_vma=False)
```

profile of v0, /device:TPU:0, one launch (start us, length us, event | category | flops | bytes accessed | tf_op | source)
XLA Modules:
  0.0 65.4 jit_solution(12571774711897113003)
XLA Ops:
  0.0 0.0 copy-start
  0.0 1.2 %copy-done = bf16[128,4096]{1,0:T(8,128)(2,1)S(1)} copy-done((bf16[128,4096]{1,0:T(8,128)(2,1)S(1)}, bf16[128,4096]{1,0:T(8,128)(2,1)}, u32[]{:S(2)}) %copy-start) | copy-done | bytes 1048600
  1.2 0.0 copy-start.1
  1.2 0.9 %copy-done.1 = bf16[128,1024]{1,0:T(8,128)(2,1)S(1)} copy-done((bf16[128,1024]{1,0:T(8,128)(2,1)S(1)}, bf16[128,1024]{1,0:T(8,128)(2,1)}, u32[]{:S(2)}) %copy-start.1) | copy-done | bytes 262168
  2.2 0.0 copy-start.2
  2.2 0.9 %copy-done.2 = bf16[128,1024]{1,0:T(8,128)(2,1)S(1)} copy-done((bf16[128,1024]{1,0:T(8,128)(2,1)S(1)}, bf16[128,1024]{1,0:T(8,128)(2,1)}, u32[]{:S(2)}) %copy-start.2) | copy-done | bytes 262168
  3.1 0.0 copy-start.3
  3.1 0.7 copy-done.3
  3.8 60.6 %attention.1 = bf16[128,4096]{1,0:T(8,128)(2,1)S(1)} custom-call(s32[64]{0:T(128)S(1)} %copy-done.3, bf16[128,4096]{1,0:T(8,128)(2,1)S(1)} %copy-done, bf16[128,1024]{1,0:T(8,128)(2,1)S(1)} %copy-done.1, bf16[128,1024]{1,0:T(8,128)(2,1)S(1)} %copy-done.2), custom_call_target="tpu_custom_call" | custom-call | tf_op jit(solution)/shard_map/attention/pallas_call | solution.py:300
  64.4 1.0 %copy.6 = bf16[128,4096]{1,0:T(8,128)(2,1)} copy(bf16[128,4096]{1,0:T(8,128)(2,1)S(1)} %attention.1) | data formatting | bytes 2097152
Async XLA Ops:
  0.0 1.2 %copy-start = (bf16[128,4096]{1,0:T(8,128)(2,1)S(1)}, bf16[128,4096]{1,0:T(8,128)(2,1)}, u32[]{:S(2)}) copy-start(bf16[128,4096]{1,0:T(8,128)(2,1)} %q_ref.1) | copy-start | bytes 3145732
  1.2 0.9 %copy-start.1 = (bf16[128,1024]{1,0:T(8,128)(2,1)S(1)}, bf16[128,1024]{1,0:T(8,128)(2,1)}, u32[]{:S(2)}) copy-start(bf16[128,1024]{1,0:T(8,128)(2,1)} %k_ref.1) | copy-start | bytes 786436
  2.2 0.9 %copy-start.2 = (bf16[128,1024]{1,0:T(8,128)(2,1)S(1)}, bf16[128,1024]{1,0:T(8,128)(2,1)}, u32[]{:S(2)}) copy-start(bf16[128,1024]{1,0:T(8,128)(2,1)} %v_ref.1) | copy-start | bytes 786436
  3.1 0.7 %copy-start.3 = (s32[64]{0:T(128)S(1)}, s32[64]{0:T(128)}, u32[]{:S(2)}) copy-start(s32[64]{0:T(128)} %lens_ref.1) | copy-start | bytes 772
where the time goes:
time: 65.6 us; the launch traced here: 65.4 us
  Pallas kernels  60.6 us (92%)
  local copies, waits for them, and re-layouts  4.75 us (7%)
    pallas_call x1, Pallas kernels, on_device(): pl.pallas_call(kernel, out_shape=jax.ShapeDtypeStruct(packed_query_rows.s...  60.6 us
    unnamed x9, local copies, waits for them, and re-layouts  4.75 us

commit v1 on v0

--- a/solution.py
+++ b/solution.py
@@ -19,12 +19,12 @@
 HIDDEN = -1e30
 MESH = pl.DeviceIdType.MESH
 RELAY_FROM = 3
-WIDE = 256
+SLAB = 256
 
 
 def kernel(
     lens_ref, q_ref, k_ref, v_ref, o_ref,
-    qb, kvb, relay, feat_q, feat_k, s_scr, p_scr, ob,
+    qb, kvb, relay, feat_q, feat_k, ob,
     q_send, q_recv, k_send, k_recv, v_send, v_recv,
     x1_send, x1_recv, x2_send, x2_recv, relay_send, relay_recv, o_send, o_recv,
 ):
@@ -42,12 +42,10 @@
 
     ahead = lax.rem(d + 2, 32)
     behind = lax.rem(d + 30, 32)
-    relay_to = chip(y, x - 1)
-    relay_source = chip(y, x + 1)
-    crossing = jnp.where((x == 1) | (x == 2), 1, 0)
-    final_to = chip(y + crossing, x - 1)
-    sender_crossing = jnp.where((x == 0) | (x == 1), 1, 0)
-    final_from = chip(y - sender_crossing, x + 1)
+    relay_to = chip(y + jnp.where(x >= 2, 1, 0), x - 1)
+    relay_source = chip(y - jnp.where((x == 1) | (x == 2), 1, 0), x + 1)
+    final_to = chip(y, x - 1)
+    final_from = chip(y, x + 1)
 
     def column(g):
         return {"head": lax.div(g, 2), "doc": c * 2 + lax.rem(g, 2)}
@@ -214,6 +212,8 @@
 
     ones = jnp.ones(((REACH + 1) * TILE, 128), jnp.bfloat16)
     span = (REACH + 1) * TILE
+    causal = lax.broadcasted_iota(jnp.int32, (TILE, TILE), 1) <= lax.broadcasted_iota(
+        jnp.int32, (TILE, TILE), 0)
 
     def attend(t, _):
         j = CHIP_TILES - 1 - t
@@ -224,28 +224,25 @@
         left = jnp.concatenate(
             [queries[:, h * HEAD_SIZE:(h + 1) * HEAD_SIZE] for h in range(GROUP)], axis=0)
         left = jnp.concatenate([left, jnp.concatenate([features] * GROUP, axis=0)], axis=1)
-        highest = None
-        for at in range(0, span, WIDE):
-            width = min(WIDE, span - at)
-            part = pl.ds(pl.multiple_of(j * TILE + at, TILE), width)
-            right = jnp.concatenate([kvb[0, part, :], feat_k[part, :]], axis=1)
-            s = lax.dot_general(
-                left, right, (((1,), (1,)), ((), ())), preferred_element_type=jnp.float32)
-            if at + width == span:
-                row = lax.rem(lax.broadcasted_iota(jnp.int32, s.shape, 0), TILE)
-                col = lax.broadcasted_iota(jnp.int32, s.shape, 1) - (width - TILE)
-                s = jnp.where(col <= row, s, HIDDEN)
-            s_scr[:, at:at + width] = s
-            for g in range(0, width, 128):
-                piece = s[:, g:g + 128]
-                highest = piece if highest is None else jnp.maximum(highest, piece)
-        highest = jnp.max(highest, axis=1, keepdims=True)
-        for at in range(0, span, WIDE):
-            width = min(WIDE, span - at)
-            p = jnp.exp2((s_scr[:, at:at + width] - highest) * SCALE)
-            p_scr[:, at:at + width] = p.astype(jnp.bfloat16)
-        values = jnp.concatenate([kvb[1, rows(j, REACH + 1), :], ones], axis=1)
-        summed = jnp.dot(p_scr[...], values, preferred_element_type=jnp.float32)
+        window = rows(j, REACH + 1)
+        right = jnp.concatenate([kvb[0, window, :], feat_k[window, :]], axis=1)
+        values = jnp.concatenate([kvb[1, window, :], ones], axis=1)
+        slabs = [
+            lax.dot_general(
+                left[i:i + SLAB], right, (((1,), (1,)), ((), ())), preferred_element_type=jnp.float32)
+            for i in range(0, GROUP * TILE, SLAB)]
+        parts = []
+        for i in range(0, GROUP * TILE, TILE):
+            s = slabs[i // SLAB][i % SLAB:i % SLAB + TILE]
+            s = jnp.concatenate(
+                [s[:, :span - TILE], jnp.where(causal, s[:, span - TILE:], HIDDEN)], axis=1)
+            highest = s[:, :128]
+            for g in range(128, span, 128):
+                highest = jnp.maximum(highest, s[:, g:g + 128])
+            highest = jnp.max(highest, axis=1, keepdims=True)
+            weights = jnp.exp2((s - highest) * SCALE).astype(jnp.bfloat16)
+            parts.append(jnp.dot(weights, values, preferred_element_type=jnp.float32))
+        summed = jnp.concatenate(parts, axis=0)
         out = (summed[:, :HEAD_SIZE] / summed[:, HEAD_SIZE:]).astype(jnp.bfloat16)
         for h in range(GROUP):
             ob[j, :, h * HEAD_SIZE:(h + 1) * HEAD_SIZE] = out[h * TILE:(h + 1) * TILE]
@@ -296,7 +293,6 @@
     bf16, f32 = jnp.bfloat16, jnp.float32
     dma = pltpu.SemaphoreType.DMA((8,))
     window = WINDOW_TILES * TILE
-    span = (REACH + 1) * TILE
     return pl.pallas_call(
         kernel,
         out_shape=jax.ShapeDtypeStruct(packed_query_rows.shape, bf16),
@@ -308,12 +304,10 @@
             pltpu.VMEM((CHIP_TILES - RELAY_FROM, 2, TILE, HEAD_SIZE), bf16),
             pltpu.VMEM((CHIP_TILES * TILE, 128), bf16),
             pltpu.VMEM((window, 128), bf16),
-            pltpu.VMEM((GROUP * TILE, span), f32),
-            pltpu.VMEM((GROUP * TILE, span), bf16),
             pltpu.VMEM((CHIP_TILES, TILE, GROUP * HEAD_SIZE), bf16),
         ] + [dma] * 14,
         compiler_params=pltpu.CompilerParams(
-            collective_id=0, has_side_effects=True, vmem_limit_bytes=40 * 1024 * 1024),
+            collective_id=0, has_side_effects=True, vmem_limit_bytes=60 * 1024 * 1024),
         name="attention",
     )(doc_lengths, packed_query_rows, packed_key_rows, packed_value_rows)
 

time: 65.6 us -> 49.4 us (0.75)
  Pallas kernels: 60.6 us -> 47 us
  local copies, waits for them, and re-layouts: 4.75 us -> 2.29 us
    pallas_call x1, Pallas kernels: 60.6 us -> 47 us  [on_device(): pl.pallas_call(kernel, out_shape=jax.ShapeDtypeStruct(packed_query_rows.s...]
    unnamed x9 -> x1, local copies, waits for them, and re-layouts: 4.75 us -> 2.29 us
where the time goes in v1:
time: 49.4 us; the launch traced here: 49.3 us
  Pallas kernels  47 us (95%)
  local copies, waits for them, and re-layouts  2.29 us (5%)
    pallas_call x1, Pallas kernels, on_device(): pl.pallas_call(kernel, out_shape=jax.ShapeDtypeStruct(packed_query_rows.s...  47 us
    unnamed x1, local copies, waits for them, and re-layouts  2.29 us

profile of v1, /device:TPU:0, one launch (start us, length us, event | category | flops | bytes accessed | tf_op | source)
XLA Modules:
  0.0 49.3 jit_solution(2384706404008060883)
XLA Ops:
  0.0 47.0 %attention.1 = bf16[128,4096]{1,0:T(8,128)(2,1)} custom-call(s32[64]{0:T(128)} %lens_ref.1, bf16[128,4096]{1,0:T(8,128)(2,1)} %q_ref.1, bf16[128,1024]{1,0:T(8,128)(2,1)} %k_ref.1, bf16[128,1024]{1,0:T(8,128)(2,1)} %v_ref.1), custom_call_target="tpu_custom_call" | custom-call | tf_op jit(solution)/shard_map/attention/pallas_call | solution.py:296
  47.0 2.3 %copy.6 = bf16[128,4096]{1,0:T(8,128)(2,1)} copy(bf16[128,4096]{1,0:T(8,128)(2,1)} %attention.1) | data formatting | bytes 2097152

commit v2 on v1

v2 whole, which is shorter than its diff:
```python
import functools
import math

import jax
import jax.numpy as jnp
from jax import lax
from jax.experimental import pallas as pl
from jax.experimental.pallas import tpu as pltpu
from jax.sharding import PartitionSpec as P

HEAD_SIZE = 128
GROUP = 4
TILE = 128
CHIP_TILES = 8
WINDOW_TILES = 24
REACH = 16
DOCS = 64
SCALE = math.log2(math.e) / math.sqrt(HEAD_SIZE)
HIDDEN = -1e30
MESH = pl.DeviceIdType.MESH
RELAYED = 5
HALF = 2 * HEAD_SIZE
CHIPS = 16
NEAREST = ((0, 0), (0, 1), (1, 0), (3, 0), (1, 1), (3, 1), (2, 0), (2, 1))
SLAB = 256


def kernel(
    lens_ref, q_ref, k_ref, v_ref, o_ref,
    qb, kvb, relay, feat_q, feat_k, ob,
    q_send, q_recv, k_send, k_recv, v_send, v_recv,
    x1_send, x1_recv, x2_send, x2_recv, relay_send, relay_recv, final_send, o_send, o_recv,
):
    z = lax.axis_index("head")
    d = lax.axis_index("doc")
    core = lax.rem(d, 2)
    c = lax.div(d, 2)
    x = lax.rem(c, 4)
    y = lax.div(c, 4)
    my_tile = core * 4 + z
    my_head = z * 2 + core

    def chip(yy, xx):
        return (lax.rem(yy + 4, 4) * 4 + lax.rem(xx + 4, 4)) * 2 + core

    ahead = lax.rem(d + 2, 32)
    behind = lax.rem(d + 30, 32)
    relay_to = chip(y + jnp.where(x >= 2, 1, 0), x - 1)
    relay_source = chip(y - jnp.where((x == 1) | (x == 2), 1, 0), x + 1)
    final_to = chip(y, x - 1)
    final_from = chip(y, x + 1)

    def column(g):
        return {"head": lax.div(g, 2), "doc": c * 2 + lax.rem(g, 2)}

    def along(dd):
        return {"head": z, "doc": dd}

    barrier = pltpu.get_barrier_semaphore()

    def greet(i, _):
        g = lax.rem(my_head + i, 8)
        pl.semaphore_signal(barrier, inc=1, device_id=column(g), device_id_type=MESH)
        return 0

    lax.fori_loop(1, 8, greet, 0)
    for other in (behind, relay_source, final_from):
        pl.semaphore_signal(barrier, inc=1, device_id=along(other), device_id_type=MESH)
    pl.semaphore_wait(barrier, 10)

    def rows(tile, count=1):
        return pl.ds(pl.multiple_of(tile * TILE, TILE), TILE * count)

    def cols(g, width):
        return pl.ds(pl.multiple_of(g * width, width), width)

    def place(dz, dcore):
        zz, cc = lax.rem(z + dz, 4), lax.rem(core + dcore, 2)
        return zz * 2 + cc, cc * 4 + zz

    def k_copy(g, tile):
        return pltpu.make_async_remote_copy(
            src_ref=k_ref.at[:, cols(g, HEAD_SIZE)],
            dst_ref=kvb.at[0, rows(REACH + tile), :],
            send_sem=k_send.at[g], recv_sem=k_recv.at[tile],
            device_id=column(g), device_id_type=MESH)

    def v_copy(g, tile):
        return pltpu.make_async_remote_copy(
            src_ref=v_ref.at[:, cols(g, HEAD_SIZE)],
            dst_ref=kvb.at[1, rows(REACH + tile), :],
            send_sem=v_send.at[g], recv_sem=v_recv.at[tile],
            device_id=column(g), device_id_type=MESH)

    def q_copy(g, tile, half):
        return pltpu.make_async_remote_copy(
            src_ref=q_ref.at[:, cols(g * 2 + half, HALF)],
            dst_ref=qb.at[half, tile],
            send_sem=q_send.at[half, g], recv_sem=q_recv.at[half, tile],
            device_id=column(g), device_id_type=MESH)

    def x1_copy(j):
        return pltpu.make_async_remote_copy(
            src_ref=kvb.at[:, rows(16 + j), :],
            dst_ref=kvb.at[:, rows(8 + j), :],
            send_sem=x1_send.at[j], recv_sem=x1_recv.at[j],
            device_id=along(ahead), device_id_type=MESH)

    def x2_copy(j):
        return pltpu.make_async_remote_copy(
            src_ref=kvb.at[:, rows(8 + j), :],
            dst_ref=kvb.at[:, rows(j), :],
            send_sem=x2_send.at[j], recv_sem=x2_recv.at[j],
            device_id=along(ahead), device_id_type=MESH)

    def relay_copy(j, slot):
        return pltpu.make_async_remote_copy(
            src_ref=kvb.at[:, rows(16 + j), :],
            dst_ref=relay.at[slot],
            send_sem=relay_send.at[slot], recv_sem=relay_recv.at[slot],
            device_id=along(relay_to), device_id_type=MESH)

    def final_copy(j, slot):
        return pltpu.make_async_remote_copy(
            src_ref=relay.at[slot],
            dst_ref=kvb.at[:, rows(j), :],
            send_sem=final_send.at[slot], recv_sem=x2_recv.at[j],
            device_id=along(final_to), device_id_type=MESH)

    def o_copy(g, tile, half):
        target = {"head": lax.rem(tile, 4), "doc": c * 2 + lax.div(tile, 4)}
        return pltpu.make_async_remote_copy(
            src_ref=ob.at[half, tile],
            dst_ref=o_ref.at[:, cols(g * 2 + half, HALF)],
            send_sem=o_send.at[half, tile], recv_sem=o_recv.at[half, g],
            device_id=target, device_id_type=MESH)

    sends_one = c < CHIPS - 1
    sends_two = (c < CHIPS - 1) & (c > 0)
    starts_relay = c < CHIPS - 2
    is_relay = y * 4 + lax.rem(x + 3, 4) >= 2
    takes_one = c > 0
    takes_two = c > 1

    pltpu.make_async_copy(
        k_ref.at[:, cols(my_head, HEAD_SIZE)], kvb.at[0, rows(REACH + my_tile), :], k_recv.at[my_tile]
    ).start()
    pltpu.make_async_copy(
        v_ref.at[:, cols(my_head, HEAD_SIZE)], kvb.at[1, rows(REACH + my_tile), :], v_recv.at[my_tile]
    ).start()
    for at in NEAREST[1:]:
        g, _ = place(*at)
        k_copy(g, my_tile).start()
        v_copy(g, my_tile).start()
    for half in range(2):
        pltpu.make_async_copy(
            q_ref.at[:, cols(my_head * 2 + half, HALF)], qb.at[half, my_tile], q_recv.at[half, my_tile]
        ).start()
        for at in NEAREST[1:]:
            g, _ = place(*at)
            q_copy(g, my_tile, half).start()

    @pl.when(c == 0)
    def _():
        kvb[:, 0:REACH * TILE, :] = jnp.zeros((2, REACH * TILE, HEAD_SIZE), jnp.bfloat16)

    @pl.when(c == 1)
    def _():
        kvb[:, 0:CHIP_TILES * TILE, :] = jnp.zeros((2, CHIP_TILES * TILE, HEAD_SIZE), jnp.bfloat16)

    lane = lax.broadcasted_iota(jnp.int32, (1, 128), 1)

    def add_document(i, bounds):
        first, end = bounds
        length = lens_ref[i]
        return first + jnp.where(lane > i, length, 0), end + jnp.where(lane >= i, length, 0)

    zero = jnp.zeros((1, 128), jnp.int32)
    first, end = lax.fori_loop(0, DOCS, add_document, (zero, zero))
    first = jnp.where(lane == DOCS, -(1 << 30), first)
    end = jnp.where(lane == DOCS, 0, end)
    line = lax.broadcasted_iota(jnp.int32, (TILE, 128), 0)

    def member(tile):
        token = line + (c * CHIP_TILES - REACH + tile) * TILE
        return (token >= first) & (token < end)

    def key_features(tile, _):
        feat_k[rows(tile), :] = jnp.where(member(tile), 1.0, 0.0).astype(jnp.bfloat16)
        return 0

    def query_features(tile, _):
        feat_q[rows(tile), :] = jnp.where(member(tile + REACH), 0.0, HIDDEN).astype(jnp.bfloat16)
        return 0

    lax.fori_loop(0, WINDOW_TILES, key_features, 0)
    lax.fori_loop(0, CHIP_TILES, query_features, 0)

    for r, at in enumerate(NEAREST):
        _, j = place(*at)
        k_copy(my_head, j).wait_recv()
        v_copy(my_head, j).wait_recv()

        @pl.when(sends_one)
        def _():
            x1_copy(j).start()

        if r < RELAYED:
            @pl.when(starts_relay)
            def _():
                relay_copy(j, r).start()

    for r, at in enumerate(NEAREST):
        _, j = place(*at)

        if r < RELAYED:
            @pl.when(is_relay)
            def _():
                relay_copy(j, r).wait_recv()
                final_copy(j, r).start()

        @pl.when(takes_one)
        def _():
            x1_copy(j).wait_recv()

        if r >= RELAYED:
            @pl.when(sends_two)
            def _():
                x2_copy(j).start()

    ones = jnp.ones(((REACH + 1) * TILE, 128), jnp.bfloat16)
    span = (REACH + 1) * TILE
    causal = lax.broadcasted_iota(jnp.int32, (TILE, TILE), 1) <= lax.broadcasted_iota(
        jnp.int32, (TILE, TILE), 0)

    def attend(half, j):
        queries = qb[half, j]
        features = feat_q[rows(j), :]
        left = jnp.concatenate([queries[:, :HEAD_SIZE], queries[:, HEAD_SIZE:]], axis=0)
        left = jnp.concatenate([left, jnp.concatenate([features] * 2, axis=0)], axis=1)
        window = rows(j, REACH + 1)
        right = jnp.concatenate([kvb[0, window, :], feat_k[window, :]], axis=1)
        values = jnp.concatenate([kvb[1, window, :], ones], axis=1)
        slabs = [
            lax.dot_general(
                left[i:i + SLAB], right, (((1,), (1,)), ((), ())), preferred_element_type=jnp.float32)
            for i in range(0, 2 * TILE, SLAB)]
        parts = []
        for i in range(0, 2 * TILE, TILE):
            s = slabs[i // SLAB][i % SLAB:i % SLAB + TILE]
            s = jnp.concatenate(
                [s[:, :span - TILE], jnp.where(causal, s[:, span - TILE:], HIDDEN)], axis=1)
            highest = s[:, :128]
            for g in range(128, span, 128):
                highest = jnp.maximum(highest, s[:, g:g + 128])
            highest = jnp.max(highest, axis=1, keepdims=True)
            weights = jnp.exp2((s - highest) * SCALE).astype(jnp.bfloat16)
            parts.append(jnp.dot(weights, values, preferred_element_type=jnp.float32))
        summed = jnp.concatenate(parts, axis=0)
        out = (summed[:, :HEAD_SIZE] / summed[:, HEAD_SIZE:]).astype(jnp.bfloat16)
        for h in range(2):
            ob[half, j, :, h * HEAD_SIZE:(h + 1) * HEAD_SIZE] = out[h * TILE:(h + 1) * TILE]

        @pl.when(j != my_tile)
        def _():
            o_copy(my_head, j, half).start()

        @pl.when(j == my_tile)
        def _():
            pltpu.make_async_copy(
                ob.at[half, j], o_ref.at[:, cols(my_head * 2 + half, HALF)], o_recv.at[half, my_head]
            ).start()

    def first_half(t, _):
        j = CHIP_TILES - 1 - t
        q_copy(my_head, j, 0).wait_recv()

        @pl.when(takes_two)
        def _():
            x2_copy(j).wait_recv()

        attend(0, j)
        return 0

    def second_half(t, _):
        j = lax.rem(my_tile + 1 + t, CHIP_TILES)
        q_copy(my_head, j, 1).wait_recv()
        attend(1, j)
        return 0

    lax.fori_loop(0, CHIP_TILES, first_half, 0)
    lax.fori_loop(0, CHIP_TILES, second_half, 0)

    for r, at in enumerate(NEAREST):
        g, j = place(*at)

        @pl.when(sends_one)
        def _():
            x1_copy(j).wait_send()

        if r < RELAYED:
            @pl.when(starts_relay)
            def _():
                relay_copy(j, r).wait_send()

            @pl.when(is_relay)
            def _():
                final_copy(j, r).wait_send()
        else:
            @pl.when(sends_two)
            def _():
                x2_copy(j).wait_send()

        if r > 0:
            k_copy(g, my_tile).wait_send()
            v_copy(g, my_tile).wait_send()
        for half in range(2):
            if r > 0:
                q_copy(g, my_tile, half).wait_send()
                o_copy(my_head, j, half).wait_send()
            o_copy(g, my_tile, half).wait_recv()


def on_device(packed_query_rows, packed_key_rows, packed_value_rows, doc_lengths):
    anywhere = pl.BlockSpec(memory_space=pl.ANY)
    bf16, f32 = jnp.bfloat16, jnp.float32
    dma = pltpu.SemaphoreType.DMA((CHIP_TILES,))
    halves = pltpu.SemaphoreType.DMA((2, CHIP_TILES))
    window = WINDOW_TILES * TILE
    return pl.pallas_call(
        kernel,
        out_shape=jax.ShapeDtypeStruct(packed_query_rows.shape, bf16),
        in_specs=[pl.BlockSpec(memory_space=pltpu.SMEM), anywhere, anywhere, anywhere],
        out_specs=anywhere,
        scratch_shapes=[
            pltpu.VMEM((2, CHIP_TILES, TILE, HALF), bf16),
            pltpu.VMEM((2, window, HEAD_SIZE), bf16),
            pltpu.VMEM((RELAYED, 2, TILE, HEAD_SIZE), bf16),
            pltpu.VMEM((CHIP_TILES * TILE, 128), bf16),
            pltpu.VMEM((window, 128), bf16),
            pltpu.VMEM((2, CHIP_TILES, TILE, HALF), bf16),
        ] + [halves] * 2 + [dma] * 11 + [halves] * 2,
        compiler_params=pltpu.CompilerParams(
            collective_id=0, has_side_effects=True, vmem_limit_bytes=60 * 1024 * 1024),
        name="attention",
    )(doc_lengths, packed_query_rows, packed_key_rows, packed_value_rows)


def solution(mesh):
    token = P(("doc", "head"), None)
    return jax.shard_map(
        on_device, mesh=mesh, in_specs=(token, token, token, P()), out_specs=token, check_vma=False)
```

time: 49.4 us -> 47.9 us (0.970)
  the two profiles are of different devices: /device:TPU:0 before, /device:TPU:24 now
where the time goes in v2:
time: 47.9 us; the launch traced here: 47.8 us
  Pallas kernels  45.5 us (95%)
  local copies, waits for them, and re-layouts  2.29 us (5%)
    pallas_call x1, Pallas kernels, on_device(): pl.pallas_call(kernel, out_shape=jax.ShapeDtypeStruct(packed_query_rows.s...  45.5 us
    unnamed x1, local copies, waits for them, and re-layouts  2.29 us

profile of v2, /device:TPU:24, one launch (start us, length us, event | category | flops | bytes accessed | tf_op | source)
XLA Modules:
  0.0 47.8 jit_solution(17151297613428520703)
XLA Ops:
  0.0 45.5 %attention.1 = bf16[128,4096]{1,0:T(8,128)(2,1)} custom-call(s32[64]{0:T(128)} %lens_ref.1, bf16[128,4096]{1,0:T(8,128)(2,1)} %q_ref.1, bf16[128,1024]{1,0:T(8,128)(2,1)} %k_ref.1, bf16[128,1024]{1,0:T(8,128)(2,1)} %v_ref.1), custom_call_target="tpu_custom_call" | custom-call | tf_op jit(solution)/shard_map/attention/pallas_call | solution.py:330
  45.5 2.3 %copy.6 = bf16[128,4096]{1,0:T(8,128)(2,1)} copy(bf16[128,4096]{1,0:T(8,128)(2,1)} %attention.1) | data formatting | bytes 2097152

commit v3 on v2

--- a/solution.py
+++ b/solution.py
@@ -9,7 +9,6 @@
 from jax.sharding import PartitionSpec as P
 
 HEAD_SIZE = 128
-GROUP = 4
 TILE = 128
 CHIP_TILES = 8
 WINDOW_TILES = 24
@@ -18,16 +17,15 @@
 SCALE = math.log2(math.e) / math.sqrt(HEAD_SIZE)
 HIDDEN = -1e30
 MESH = pl.DeviceIdType.MESH
-RELAYED = 5
+RELAYED = (7, 6, 5, 3, 1)
 HALF = 2 * HEAD_SIZE
 CHIPS = 16
 NEAREST = ((0, 0), (0, 1), (1, 0), (3, 0), (1, 1), (3, 1), (2, 0), (2, 1))
-SLAB = 256
 
 
 def kernel(
     lens_ref, q_ref, k_ref, v_ref, o_ref,
-    qb, kvb, relay, feat_q, feat_k, ob,
+    qb, kvb, kt, relay, feat_q, ob,
     q_send, q_recv, k_send, k_recv, v_send, v_recv,
     x1_send, x1_recv, x2_send, x2_recv, relay_send, relay_recv, final_send, o_send, o_recv,
 ):
@@ -113,18 +111,21 @@
             send_sem=x2_send.at[j], recv_sem=x2_recv.at[j],
             device_id=along(ahead), device_id_type=MESH)
 
-    def relay_copy(j, slot):
+    def goes_round(j):
+        return (lax.rem(j, 2) == 1) | (j == 6)
+
+    def relay_copy(j):
         return pltpu.make_async_remote_copy(
             src_ref=kvb.at[:, rows(16 + j), :],
-            dst_ref=relay.at[slot],
-            send_sem=relay_send.at[slot], recv_sem=relay_recv.at[slot],
+            dst_ref=relay.at[j],
+            send_sem=relay_send.at[j], recv_sem=relay_recv.at[j],
             device_id=along(relay_to), device_id_type=MESH)
 
-    def final_copy(j, slot):
-        return pltpu.make_async_remote_copy(
-            src_ref=relay.at[slot],
+    def final_copy(j):
+        return pltpu.make_async_remote_copy(
+            src_ref=relay.at[j],
             dst_ref=kvb.at[:, rows(j), :],
-            send_sem=final_send.at[slot], recv_sem=x2_recv.at[j],
+            send_sem=final_send.at[j], recv_sem=x2_recv.at[j],
             device_id=along(final_to), device_id_type=MESH)
 
     def o_copy(g, tile, half):
@@ -186,7 +187,7 @@
         return (token >= first) & (token < end)
 
     def key_features(tile, _):
-        feat_k[rows(tile), :] = jnp.where(member(tile), 1.0, 0.0).astype(jnp.bfloat16)
+        kt[HEAD_SIZE:, rows(tile)] = jnp.where(member(tile), 1.0, 0.0).astype(jnp.bfloat16).T
         return 0
 
     def query_features(tile, _):
@@ -195,6 +196,9 @@
 
     lax.fori_loop(0, WINDOW_TILES, key_features, 0)
     lax.fori_loop(0, CHIP_TILES, query_features, 0)
+
+    def turn(tile):
+        kt[:HEAD_SIZE, rows(tile)] = kvb[0, rows(tile), :].T
 
     for r, at in enumerate(NEAREST):
         _, j = place(*at)
@@ -205,92 +209,94 @@
         def _():
             x1_copy(j).start()
 
-        if r < RELAYED:
-            @pl.when(starts_relay)
-            def _():
-                relay_copy(j, r).start()
+        @pl.when(starts_relay & goes_round(j))
+        def _():
+            relay_copy(j).start()
+
+        turn(REACH + j)
 
     for r, at in enumerate(NEAREST):
         _, j = place(*at)
 
-        if r < RELAYED:
+        @pl.when(takes_one)
+        def _():
+            x1_copy(j).wait_recv()
+
+        @pl.when(sends_two & jnp.logical_not(goes_round(j)))
+        def _():
+            x2_copy(j).start()
+
+        if r >= CHIP_TILES - len(RELAYED):
             @pl.when(is_relay)
             def _():
-                relay_copy(j, r).wait_recv()
-                final_copy(j, r).start()
-
-        @pl.when(takes_one)
-        def _():
-            x1_copy(j).wait_recv()
-
-        if r >= RELAYED:
-            @pl.when(sends_two)
-            def _():
-                x2_copy(j).start()
+                relayed = RELAYED[r - CHIP_TILES + len(RELAYED)]
+                relay_copy(relayed).wait_recv()
+                final_copy(relayed).start()
+
+        turn(CHIP_TILES + j)
 
     ones = jnp.ones(((REACH + 1) * TILE, 128), jnp.bfloat16)
     span = (REACH + 1) * TILE
     causal = lax.broadcasted_iota(jnp.int32, (TILE, TILE), 1) <= lax.broadcasted_iota(
         jnp.int32, (TILE, TILE), 0)
 
-    def attend(half, j):
-        queries = qb[half, j]
-        features = feat_q[rows(j), :]
-        left = jnp.concatenate([queries[:, :HEAD_SIZE], queries[:, HEAD_SIZE:]], axis=0)
-        left = jnp.concatenate([left, jnp.concatenate([features] * 2, axis=0)], axis=1)
-        window = rows(j, REACH + 1)
-        right = jnp.concatenate([kvb[0, window, :], feat_k[window, :]], axis=1)
-        values = jnp.concatenate([kvb[1, window, :], ones], axis=1)
-        slabs = [
-            lax.dot_general(
-                left[i:i + SLAB], right, (((1,), (1,)), ((), ())), preferred_element_type=jnp.float32)
-            for i in range(0, 2 * TILE, SLAB)]
-        parts = []
-        for i in range(0, 2 * TILE, TILE):
-            s = slabs[i // SLAB][i % SLAB:i % SLAB + TILE]
-            s = jnp.concatenate(
-                [s[:, :span - TILE], jnp.where(causal, s[:, span - TILE:], HIDDEN)], axis=1)
-            highest = s[:, :128]
-            for g in range(128, span, 128):
-                highest = jnp.maximum(highest, s[:, g:g + 128])
-            highest = jnp.max(highest, axis=1, keepdims=True)
-            weights = jnp.exp2((s - highest) * SCALE).astype(jnp.bfloat16)
-            parts.append(jnp.dot(weights, values, preferred_element_type=jnp.float32))
-        summed = jnp.concatenate(parts, axis=0)
-        out = (summed[:, :HEAD_SIZE] / summed[:, HEAD_SIZE:]).astype(jnp.bfloat16)
-        for h in range(2):
-            ob[half, j, :, h * HEAD_SIZE:(h + 1) * HEAD_SIZE] = out[h * TILE:(h + 1) * TILE]
-
-        @pl.when(j != my_tile)
-        def _():
-            o_copy(my_head, j, half).start()
-
-        @pl.when(j == my_tile)
-        def _():
-            pltpu.make_async_copy(
-                ob.at[half, j], o_ref.at[:, cols(my_head * 2 + half, HALF)], o_recv.at[half, my_head]
-            ).start()
+    def scores(half, j, h):
+        queries = qb[half, j, :, h * HEAD_SIZE:(h + 1) * HEAD_SIZE]
+        left = jnp.concatenate([queries, feat_q[rows(j), :]], axis=1)
+        s = jnp.dot(left, kt[:, rows(j, REACH + 1)], preferred_element_type=jnp.float32)
+        return jnp.concatenate(
+            [s[:, :span - TILE], jnp.where(causal, s[:, span - TILE:], HIDDEN)], axis=1)
+
+    def weigh(half, j, h, s):
+        highest = s[:, :128]
+        for g in range(128, span, 128):
+            highest = jnp.maximum(highest, s[:, g:g + 128])
+        highest = jnp.max(highest, axis=1, keepdims=True)
+        weights = jnp.exp2((s - highest) * SCALE).astype(jnp.bfloat16)
+        values = jnp.concatenate([kvb[1, rows(j, REACH + 1), :], ones], axis=1)
+        summed = jnp.dot(weights, values, preferred_element_type=jnp.float32)
+        out = summed[:, :HEAD_SIZE] / summed[:, HEAD_SIZE:]
+        ob[half, j, :, h * HEAD_SIZE:(h + 1) * HEAD_SIZE] = out.astype(jnp.bfloat16)
+
+    def attend(half, tiles):
+        units = [(j, h) for j in tiles for h in range(2)]
+        scored = [scores(half, j, h) for j, h in units]
+        for (j, h), s in zip(units, scored):
+            weigh(half, j, h, s)
+        for j in tiles:
+            @pl.when(j != my_tile)
+            def _():
+                o_copy(my_head, j, half).start()
+
+            @pl.when(j == my_tile)
+            def _():
+                pltpu.make_async_copy(
+                    ob.at[half, j], o_ref.at[:, cols(my_head * 2 + half, HALF)],
+                    o_recv.at[half, my_head]
+                ).start()
 
     def first_half(t, _):
-        j = CHIP_TILES - 1 - t
-        q_copy(my_head, j, 0).wait_recv()
-
-        @pl.when(takes_two)
-        def _():
-            x2_copy(j).wait_recv()
-
-        attend(0, j)
+        tiles = (CHIP_TILES - 1 - 2 * t, CHIP_TILES - 2 - 2 * t)
+        for j in tiles:
+            q_copy(my_head, j, 0).wait_recv()
+
+            @pl.when(takes_two)
+            def _():
+                x2_copy(j).wait_recv()
+
+            turn(j)
+        attend(0, tiles)
         return 0
 
     def second_half(t, _):
-        j = lax.rem(my_tile + 1 + t, CHIP_TILES)
-        q_copy(my_head, j, 1).wait_recv()
-        attend(1, j)
-        return 0
-
-    lax.fori_loop(0, CHIP_TILES, first_half, 0)
-    lax.fori_loop(0, CHIP_TILES, second_half, 0)
-
+        tiles = tuple(lax.rem(my_tile + 2 * t + n, CHIP_TILES) for n in (1, 2))
+        for j in tiles:
+            q_copy(my_head, j, 1).wait_recv()
+        attend(1, tiles)
+        return 0
+
+    lax.fori_loop(0, CHIP_TILES // 2, first_half, 0)
+    lax.fori_loop(0, CHIP_TILES // 2, second_half, 0)
     for r, at in enumerate(NEAREST):
         g, j = place(*at)
 
@@ -298,18 +304,18 @@
         def _():
             x1_copy(j).wait_send()
 
-        if r < RELAYED:
-            @pl.when(starts_relay)
-            def _():
-                relay_copy(j, r).wait_send()
-
+        @pl.when(starts_relay & goes_round(j))
+        def _():
+            relay_copy(j).wait_send()
+
+        @pl.when(sends_two & jnp.logical_not(goes_round(j)))
+        def _():
+            x2_copy(j).wait_send()
+
+        if r < len(RELAYED):
             @pl.when(is_relay)
             def _():
-                final_copy(j, r).wait_send()
-        else:
-            @pl.when(sends_two)
-            def _():
-                x2_copy(j).wait_send()
+                final_copy(RELAYED[r]).wait_send()
 
         if r > 0:
             k_copy(g, my_tile).wait_send()
@@ -335,9 +341,9 @@
         scratch_shapes=[
             pltpu.VMEM((2, CHIP_TILES, TILE, HALF), bf16),
             pltpu.VMEM((2, window, HEAD_SIZE), bf16),
-            pltpu.VMEM((RELAYED, 2, TILE, HEAD_SIZE), bf16),
+            pltpu.VMEM((2 * HEAD_SIZE, window), bf16),
+            pltpu.VMEM((CHIP_TILES, 2, TILE, HEAD_SIZE), bf16),
             pltpu.VMEM((CHIP_TILES * TILE, 128), bf16),
-            pltpu.VMEM((window, 128), bf16),
             pltpu.VMEM((2, CHIP_TILES, TILE, HALF), bf16),
         ] + [halves] * 2 + [dma] * 11 + [halves] * 2,
         compiler_params=pltpu.CompilerParams(

time: 47.9 us -> 45.1 us (0.942)
  Pallas kernels: 45.5 us -> 42.6 us
    pallas_call x1, Pallas kernels: 45.5 us -> 42.6 us  [on_device(): pl.pallas_call(kernel, out_shape=jax.ShapeDtypeStruct(packed_query_rows.s...]
where the time goes in v3:
time: 45.1 us; the launch traced here: 44.9 us
  Pallas kernels  42.6 us (94%)
  local copies, waits for them, and re-layouts  2.29 us (5%)
    pallas_call x1, Pallas kernels, on_device(): pl.pallas_call(kernel, out_shape=jax.ShapeDtypeStruct(packed_query_rows.s...  42.6 us
    unnamed x1, local copies, waits for them, and re-layouts  2.29 us

profile of v3, /device:TPU:24, one launch (start us, length us, event | category | flops | bytes accessed | tf_op | source)
XLA Modules:
  0.0 44.9 jit_solution(8305359529556773930)
XLA Ops:
  0.0 42.6 %attention.1 = bf16[128,4096]{1,0:T(8,128)(2,1)} custom-call(s32[64]{0:T(128)} %lens_ref.1, bf16[128,4096]{1,0:T(8,128)(2,1)} %q_ref.1, bf16[128,1024]{1,0:T(8,128)(2,1)} %k_ref.1, bf16[128,1024]{1,0:T(8,128)(2,1)} %v_ref.1), custom_call_target="tpu_custom_call" | custom-call | tf_op jit(solution)/shard_map/attention/pallas_call | solution.py:336
  42.6 2.3 %copy.6 = bf16[128,4096]{1,0:T(8,128)(2,1)} copy(bf16[128,4096]{1,0:T(8,128)(2,1)} %attention.1) | data formatting | bytes 2097152

commit v4 on v3

--- a/solution.py
+++ b/solution.py
@@ -20,6 +20,9 @@
 RELAYED = (7, 6, 5, 3, 1)
 HALF = 2 * HEAD_SIZE
 CHIPS = 16
+FROM_FIRST = ((0, 1), (1, 1), (3, 1), (2, 1), (1, 0), (3, 0), (2, 0))
+FROM_SECOND = ((1, 1), (3, 1), (2, 1), (0, 0), (1, 0), (3, 0), (2, 0))
+HELD = 0
 NEAREST = ((0, 0), (0, 1), (1, 0), (3, 0), (1, 1), (3, 1), (2, 0), (2, 1))
 
 
@@ -54,6 +57,18 @@
     def along(dd):
         return {"head": z, "doc": dd}
 
+    def rows(tile, count=1):
+        return pl.ds(pl.multiple_of(tile * TILE, TILE), TILE * count)
+
+    def cols(g, width):
+        return pl.ds(pl.multiple_of(g * width, width), width)
+
+    pltpu.make_async_copy(
+        k_ref.at[:, cols(my_head, HEAD_SIZE)], kvb.at[0, rows(REACH + my_tile), :], k_recv.at[my_tile]
+    ).start()
+    pltpu.make_async_copy(
+        v_ref.at[:, cols(my_head, HEAD_SIZE)], kvb.at[1, rows(REACH + my_tile), :], v_recv.at[my_tile]
+    ).start()
     barrier = pltpu.get_barrier_semaphore()
 
     def greet(i, _):
@@ -64,13 +79,44 @@
     lax.fori_loop(1, 8, greet, 0)
     for other in (behind, relay_source, final_from):
         pl.semaphore_signal(barrier, inc=1, device_id=along(other), device_id_type=MESH)
+    @pl.when(c == 0)
+    def _():
+        kvb[:, 0:REACH * TILE, :] = jnp.zeros((2, REACH * TILE, HEAD_SIZE), jnp.bfloat16)
+
+    @pl.when(c == 1)
+    def _():
+        kvb[:, 0:CHIP_TILES * TILE, :] = jnp.zeros((2, CHIP_TILES * TILE, HEAD_SIZE), jnp.bfloat16)
+
+    lane = lax.broadcasted_iota(jnp.int32, (1, 128), 1)
+
+    def add_document(i, bounds):
+        first, end = bounds
+        length = lens_ref[i]
+        return first + jnp.where(lane > i, length, 0), end + jnp.where(lane >= i, length, 0)
+
+    zero = jnp.zeros((1, 128), jnp.int32)
+    first, end = lax.fori_loop(0, DOCS, add_document, (zero, zero))
+    first = jnp.where(lane == DOCS, -(1 << 30), first)
+    end = jnp.where(lane == DOCS, 0, end)
+    line = lax.broadcasted_iota(jnp.int32, (TILE, 128), 0)
+
+    def member(tile):
+        token = line + (c * CHIP_TILES - REACH + tile) * TILE
+        return (token >= first) & (token < end)
+
+    def key_features(tile, _):
+        kt[HEAD_SIZE:, rows(tile)] = jnp.where(member(tile), 1.0, 0.0).astype(jnp.bfloat16).T
+        return 0
+
+    def query_features(tile, _):
+        feat_q[rows(tile), :] = jnp.where(member(tile + REACH), 0.0, HIDDEN).astype(jnp.bfloat16)
+        return 0
+
+    lax.fori_loop(0, WINDOW_TILES, key_features, 0)
+    lax.fori_loop(0, CHIP_TILES, query_features, 0)
+
     pl.semaphore_wait(barrier, 10)
 
-    def rows(tile, count=1):
-        return pl.ds(pl.multiple_of(tile * TILE, TILE), TILE * count)
-
-    def cols(g, width):
-        return pl.ds(pl.multiple_of(g * width, width), width)
 
     def place(dz, dcore):
         zz, cc = lax.rem(z + dz, 4), lax.rem(core + dcore, 2)
@@ -143,97 +189,88 @@
     takes_one = c > 0
     takes_two = c > 1
 
-    pltpu.make_async_copy(
-        k_ref.at[:, cols(my_head, HEAD_SIZE)], kvb.at[0, rows(REACH + my_tile), :], k_recv.at[my_tile]
-    ).start()
-    pltpu.make_async_copy(
-        v_ref.at[:, cols(my_head, HEAD_SIZE)], kvb.at[1, rows(REACH + my_tile), :], v_recv.at[my_tile]
-    ).start()
-    for at in NEAREST[1:]:
+    def turn(tile):
+        kt[:HEAD_SIZE, rows(tile)] = kvb[0, rows(tile), :].T
+
+    def pass_own(j):
+        k_copy(my_head, j).wait_recv()
+        v_copy(my_head, j).wait_recv()
+
+        @pl.when(sends_one)
+        def _():
+            x1_copy(j).start()
+
+        @pl.when(starts_relay & goes_round(j))
+        def _():
+            relay_copy(j).start()
+
+    def pass_round(j):
+        @pl.when(is_relay)
+        def _():
+            relay_copy(j).wait_recv()
+            final_copy(j).start()
+
+    def pass_on(j):
+        @pl.when(takes_one)
+        def _():
+            x1_copy(j).wait_recv()
+
+        @pl.when(sends_two & jnp.logical_not(goes_round(j)))
+        def _():
+            x2_copy(j).start()
+
+    arrivals = [my_tile]
+    for (dz0, core0), (dz1, core1) in zip(FROM_FIRST, FROM_SECOND):
+        first_core = core == 0
+        zz = lax.rem(z + jnp.where(first_core, dz0, dz1), 4)
+        arrivals.append(jnp.where(first_core, core0, core1) * 4 + zz)
+
+    def send_kv(at):
         g, _ = place(*at)
         k_copy(g, my_tile).start()
         v_copy(g, my_tile).start()
+
+    def send_q():
+        for half in range(2):
+            for at in NEAREST[1:]:
+                g, _ = place(*at)
+                q_copy(g, my_tile, half).start()
+
+    send_kv(NEAREST[1])
+
+    @pl.when(core == 1)
+    def _():
+        for at in NEAREST[2:]:
+            send_kv(at)
+
     for half in range(2):
         pltpu.make_async_copy(
             q_ref.at[:, cols(my_head * 2 + half, HALF)], qb.at[half, my_tile], q_recv.at[half, my_tile]
         ).start()
-        for at in NEAREST[1:]:
-            g, _ = place(*at)
-            q_copy(g, my_tile, half).start()
-
-    @pl.when(c == 0)
+    pass_own(my_tile)
+
+    @pl.when(core == 1)
     def _():
-        kvb[:, 0:REACH * TILE, :] = jnp.zeros((2, REACH * TILE, HEAD_SIZE), jnp.bfloat16)
-
-    @pl.when(c == 1)
-    def _():
-        kvb[:, 0:CHIP_TILES * TILE, :] = jnp.zeros((2, CHIP_TILES * TILE, HEAD_SIZE), jnp.bfloat16)
-
-    lane = lax.broadcasted_iota(jnp.int32, (1, 128), 1)
-
-    def add_document(i, bounds):
-        first, end = bounds
-        length = lens_ref[i]
-        return first + jnp.where(lane > i, length, 0), end + jnp.where(lane >= i, length, 0)
-
-    zero = jnp.zeros((1, 128), jnp.int32)
-    first, end = lax.fori_loop(0, DOCS, add_document, (zero, zero))
-    first = jnp.where(lane == DOCS, -(1 << 30), first)
-    end = jnp.where(lane == DOCS, 0, end)
-    line = lax.broadcasted_iota(jnp.int32, (TILE, 128), 0)
-
-    def member(tile):
-        token = line + (c * CHIP_TILES - REACH + tile) * TILE
-        return (token >= first) & (token < end)
-
-    def key_features(tile, _):
-        kt[HEAD_SIZE:, rows(tile)] = jnp.where(member(tile), 1.0, 0.0).astype(jnp.bfloat16).T
-        return 0
-
-    def query_features(tile, _):
-        feat_q[rows(tile), :] = jnp.where(member(tile + REACH), 0.0, HIDDEN).astype(jnp.bfloat16)
-        return 0
-
-    lax.fori_loop(0, WINDOW_TILES, key_features, 0)
-    lax.fori_loop(0, CHIP_TILES, query_features, 0)
-
-    def turn(tile):
-        kt[:HEAD_SIZE, rows(tile)] = kvb[0, rows(tile), :].T
-
-    for r, at in enumerate(NEAREST):
-        _, j = place(*at)
-        k_copy(my_head, j).wait_recv()
-        v_copy(my_head, j).wait_recv()
-
-        @pl.when(sends_one)
-        def _():
-            x1_copy(j).start()
-
-        @pl.when(starts_relay & goes_round(j))
-        def _():
-            relay_copy(j).start()
-
+        send_q()
+
+    for r, j in enumerate(arrivals[1:]):
+        pass_own(j)
+        if r == HELD:
+            @pl.when(core == 0)
+            def _():
+                for at in NEAREST[2:]:
+                    send_kv(at)
+                send_q()
+
+    for r, j in enumerate(arrivals):
         turn(REACH + j)
-
-    for r, at in enumerate(NEAREST):
-        _, j = place(*at)
-
-        @pl.when(takes_one)
-        def _():
-            x1_copy(j).wait_recv()
-
-        @pl.when(sends_two & jnp.logical_not(goes_round(j)))
-        def _():
-            x2_copy(j).start()
-
-        if r >= CHIP_TILES - len(RELAYED):
-            @pl.when(is_relay)
-            def _():
-                relayed = RELAYED[r - CHIP_TILES + len(RELAYED)]
-                relay_copy(relayed).wait_recv()
-                final_copy(relayed).start()
-
+        if r < 3:
+            pass_round(RELAYED[r])
+    for r, j in enumerate(arrivals):
+        pass_on(j)
         turn(CHIP_TILES + j)
+        if r in (2, 4):
+            pass_round(RELAYED[3 + r // 4])
 
     ones = jnp.ones(((REACH + 1) * TILE, 128), jnp.bfloat16)
     span = (REACH + 1) * TILE
@@ -289,7 +326,11 @@
         return 0
 
     def second_half(t, _):
-        tiles = tuple(lax.rem(my_tile + 2 * t + n, CHIP_TILES) for n in (1, 2))
+        outer, last = t == 0, t == 3
+        tiles = (
+            place(jnp.where(outer, 2, jnp.where(last, 0, 3)), jnp.where(t == 2, 0, 1))[1],
+            place(jnp.where(outer, 2, jnp.where(last, 0, 1)), jnp.where(t == 1, 1, 0))[1],
+        )
         for j in tiles:
             q_copy(my_head, j, 1).wait_recv()
         attend(1, tiles)

time: 45.1 us -> 43.2 us (0.958)
  Pallas kernels: 42.6 us -> 40.3 us
    pallas_call x1, Pallas kernels: 42.6 us -> 40.3 us  [on_device(): pl.pallas_call(kernel, out_shape=jax.ShapeDtypeStruct(packed_query_rows.s...]
where the time goes in v4:
time: 43.2 us; the launch traced here: 42.6 us
  Pallas kernels  40.3 us (93%)
  local copies, waits for them, and re-layouts  2.29 us (5%)
    pallas_call x1, Pallas kernels, on_device(): pl.pallas_call(kernel, out_shape=jax.ShapeDtypeStruct(packed_query_rows.s...  40.3 us
    unnamed x1, local copies, waits for them, and re-layouts  2.29 us

profile of v4, /device:TPU:24, one launch (start us, length us, event | category | flops | bytes accessed | tf_op | source)
XLA Modules:
  0.0 42.6 jit_solution(8472357745711658729)
XLA Ops:
  0.0 40.3 %attention.1 = bf16[128,4096]{1,0:T(8,128)(2,1)} custom-call(s32[64]{0:T(128)} %lens_ref.1, bf16[128,4096]{1,0:T(8,128)(2,1)} %q_ref.1, bf16[128,1024]{1,0:T(8,128)(2,1)} %k_ref.1, bf16[128,1024]{1,0:T(8,128)(2,1)} %v_ref.1), custom_call_target="tpu_custom_call" | custom-call | tf_op jit(solution)/shard_map/attention/pallas_call | solution.py:377
  40.3 2.3 %copy.6 = bf16[128,4096]{1,0:T(8,128)(2,1)} copy(bf16[128,4096]{1,0:T(8,128)(2,1)} %attention.1) | data formatting | bytes 2097152

commit v5 on v4

--- a/solution.py
+++ b/solution.py
@@ -17,11 +17,13 @@
 SCALE = math.log2(math.e) / math.sqrt(HEAD_SIZE)
 HIDDEN = -1e30
 MESH = pl.DeviceIdType.MESH
-RELAYED = (7, 6, 5, 3, 1)
+RELAYED = (7, 6, 5, 4, 2)
 HALF = 2 * HEAD_SIZE
 CHIPS = 16
 FROM_FIRST = ((0, 1), (1, 1), (3, 1), (2, 1), (1, 0), (3, 0), (2, 0))
 FROM_SECOND = ((1, 1), (3, 1), (2, 1), (0, 0), (1, 0), (3, 0), (2, 0))
+AFTER_OWN = {4: (7,), 5: (6,), 6: (5,)}
+AFTER_CHAINED = {0: (4,), 2: (2,)}
 HELD = 0
 NEAREST = ((0, 0), (0, 1), (1, 0), (3, 0), (1, 1), (3, 1), (2, 0), (2, 1))
 
@@ -79,42 +81,6 @@
     lax.fori_loop(1, 8, greet, 0)
     for other in (behind, relay_source, final_from):
         pl.semaphore_signal(barrier, inc=1, device_id=along(other), device_id_type=MESH)
-    @pl.when(c == 0)
-    def _():
-        kvb[:, 0:REACH * TILE, :] = jnp.zeros((2, REACH * TILE, HEAD_SIZE), jnp.bfloat16)
-
-    @pl.when(c == 1)
-    def _():
-        kvb[:, 0:CHIP_TILES * TILE, :] = jnp.zeros((2, CHIP_TILES * TILE, HEAD_SIZE), jnp.bfloat16)
-
-    lane = lax.broadcasted_iota(jnp.int32, (1, 128), 1)
-
-    def add_document(i, bounds):
-        first, end = bounds
-        length = lens_ref[i]
-        return first + jnp.where(lane > i, length, 0), end + jnp.where(lane >= i, length, 0)
-
-    zero = jnp.zeros((1, 128), jnp.int32)
-    first, end = lax.fori_loop(0, DOCS, add_document, (zero, zero))
-    first = jnp.where(lane == DOCS, -(1 << 30), first)
-    end = jnp.where(lane == DOCS, 0, end)
-    line = lax.broadcasted_iota(jnp.int32, (TILE, 128), 0)
-
-    def member(tile):
-        token = line + (c * CHIP_TILES - REACH + tile) * TILE
-        return (token >= first) & (token < end)
-
-    def key_features(tile, _):
-        kt[HEAD_SIZE:, rows(tile)] = jnp.where(member(tile), 1.0, 0.0).astype(jnp.bfloat16).T
-        return 0
-
-    def query_features(tile, _):
-        feat_q[rows(tile), :] = jnp.where(member(tile + REACH), 0.0, HIDDEN).astype(jnp.bfloat16)
-        return 0
-
-    lax.fori_loop(0, WINDOW_TILES, key_features, 0)
-    lax.fori_loop(0, CHIP_TILES, query_features, 0)
-
     pl.semaphore_wait(barrier, 10)
 
 
@@ -158,7 +124,7 @@
             device_id=along(ahead), device_id_type=MESH)
 
     def goes_round(j):
-        return (lax.rem(j, 2) == 1) | (j == 6)
+        return functools.reduce(jnp.logical_or, [j == tile for tile in RELAYED])
 
     def relay_copy(j):
         return pltpu.make_async_remote_copy(
@@ -232,10 +198,11 @@
 
     def send_q():
         for half in range(2):
-            for at in NEAREST[1:]:
-                g, _ = place(*at)
+            for dz, dcore in NEAREST[1:]:
+                g, _ = place(lax.rem(jnp.where(core == 0, dz, 4 - dz), 4), dcore)
                 q_copy(g, my_tile, half).start()
 
+    pass_own(my_tile)
     send_kv(NEAREST[1])
 
     @pl.when(core == 1)
@@ -247,11 +214,47 @@
         pltpu.make_async_copy(
             q_ref.at[:, cols(my_head * 2 + half, HALF)], qb.at[half, my_tile], q_recv.at[half, my_tile]
         ).start()
-    pass_own(my_tile)
 
     @pl.when(core == 1)
     def _():
         send_q()
+
+    @pl.when(c == 0)
+    def _():
+        kvb[:, 0:REACH * TILE, :] = jnp.zeros((2, REACH * TILE, HEAD_SIZE), jnp.bfloat16)
+
+    @pl.when(c == 1)
+    def _():
+        kvb[:, 0:CHIP_TILES * TILE, :] = jnp.zeros((2, CHIP_TILES * TILE, HEAD_SIZE), jnp.bfloat16)
+
+    lane = lax.broadcasted_iota(jnp.int32, (1, 128), 1)
+
+    def add_document(i, bounds):
+        first, end = bounds
+        length = lens_ref[i]
+        return first + jnp.where(lane > i, length, 0), end + jnp.where(lane >= i, length, 0)
+
+    zero = jnp.zeros((1, 128), jnp.int32)
+    first, end = lax.fori_loop(0, DOCS, add_document, (zero, zero))
+    first = jnp.where(lane == DOCS, -(1 << 30), first)
+    end = jnp.where(lane == DOCS, 0, end)
+    line = lax.broadcasted_iota(jnp.int32, (TILE, 128), 0)
+
+    def member(tile):
+        token = line + (c * CHIP_TILES - REACH + tile) * TILE
+        return (token >= first) & (token < end)
+
+    def key_features(tile, _):
+        kt[HEAD_SIZE:, rows(tile)] = jnp.where(member(tile), 1.0, 0.0).astype(jnp.bfloat16).T
+        return 0
+
+    def query_features(tile, _):
+        feat_q[rows(tile), :] = jnp.where(member(tile + REACH), 0.0, HIDDEN).astype(jnp.bfloat16)
+        return 0
+
+    def mark_documents():
+        lax.fori_loop(0, WINDOW_TILES, key_features, 0)
+        lax.fori_loop(0, CHIP_TILES, query_features, 0)
 
     for r, j in enumerate(arrivals[1:]):
         pass_own(j)
@@ -261,16 +264,18 @@
                 for at in NEAREST[2:]:
                     send_kv(at)
                 send_q()
+        if r == 0:
+            mark_documents()
+        for tile in AFTER_OWN.get(r, ()):
+            pass_round(tile)
 
     for r, j in enumerate(arrivals):
         turn(REACH + j)
-        if r < 3:
-            pass_round(RELAYED[r])
     for r, j in enumerate(arrivals):
         pass_on(j)
         turn(CHIP_TILES + j)
-        if r in (2, 4):
-            pass_round(RELAYED[3 + r // 4])
+        for tile in AFTER_CHAINED.get(r, ()):
+            pass_round(tile)
 
     ones = jnp.ones(((REACH + 1) * TILE, 128), jnp.bfloat16)
     span = (REACH + 1) * TILE

time: 43.2 us -> 43.1 us (level)
  no operation moved by 1% of the time
where the time goes in v5:
time: 43.1 us; the launch traced here: 42.5 us
  Pallas kernels  40.2 us (93%)
  local copies, waits for them, and re-layouts  2.29 us (5%)
    pallas_call x1, Pallas kernels, on_device(): pl.pallas_call(kernel, out_shape=jax.ShapeDtypeStruct(packed_query_rows.s...  40.2 us
    unnamed x1, local copies, waits for them, and re-layouts  2.29 us

profile of v5, /device:TPU:24, one launch (start us, length us, event | category | flops | bytes accessed | tf_op | source)
XLA Modules:
  0.0 42.5 jit_solution(4628741213648869006)
XLA Ops:
  0.0 40.2 %attention.1 = bf16[128,4096]{1,0:T(8,128)(2,1)} custom-call(s32[64]{0:T(128)} %lens_ref.1, bf16[128,4096]{1,0:T(8,128)(2,1)} %q_ref.1, bf16[128,1024]{1,0:T(8,128)(2,1)} %k_ref.1, bf16[128,1024]{1,0:T(8,128)(2,1)} %v_ref.1), custom_call_target="tpu_custom_call" | custom-call | tf_op jit(solution)/shard_map/attention/pallas_call | solution.py:382
  40.3 2.3 %copy.6 = bf16[128,4096]{1,0:T(8,128)(2,1)} copy(bf16[128,4096]{1,0:T(8,128)(2,1)} %attention.1) | data formatting | bytes 2097152
